TPU v7x, 32 devices: a whole 2x2x4 slice. The times are simulated.
32 devices in a mesh: section: 2 (over x), fsdp: 8 (over z, y), dp: 2 (over core).
Axes of the slice: x: 2, y: 2, z: 4, core: 2. Of those that a mesh axis runs over, the one named last changes fastest.
Arguments:
- hidden: bfloat16 [4, 512, 8192], P(('section', 'dp'), 'fsdp'), may hold values from -7 to 7
- cotangent: bfloat16 [4, 512, 8192], P(('section', 'dp'), None, 'fsdp'), may hold values from -6 to 6
- seg_ids: int32 [4, 512], P(('section', 'dp')), may hold values from 0 to 8, as said below
- advantage: float32 [4, 8], P(('section', 'dp')), may hold values from -4 to 4
- w_query: bfloat16 [8192, 8192], P('fsdp'), may hold values from -6 to 6
- w_key: bfloat16 [8192, 1024], P('fsdp'), may hold values from -6 to 6
- w_value: bfloat16 [8192, 1024], P('fsdp'), may hold values from -6 to 6
Outputs:
- rollout_query: bfloat16 [8192, 8192], P(None, 'fsdp')
- rollout_key: bfloat16 [8192, 1024], P(None, 'fsdp')
- rollout_value: bfloat16 [8192, 1024], P(None, 'fsdp')
Inputs may be any that keep to these rules, and one draw needn't show every extreme that they name: `seg_ids`: in each block ids never fall; each id below 8 covers 1 to 64 positions, one of them exactly 64, and every id below 8 appears; id 8 marks padding at the block's end.
All inputs are finite; a program needn't handle non-finite values.
Results may differ from a plain program's by a relative error of at most 0.015.
The roundings to bfloat16 on the way count: a program that leaves them out, or rounds other values in their place, can miss the bound.
Values may be sent and summed in bfloat16 or wider, within the bound.
A program may use at most 192 MiB of HBM per device.

v0:
```python
import jax
import jax.numpy as jnp
from jax import lax
from jax.sharding import PartitionSpec as P

D = 8192
H = 64
KVH = 8
HD = 128
RESP = 8


step_rate = 200.0
rope_base = 1000000.0
norm_eps = 1e-06
masked_score = -1e30


def rotate(field, cosine_table, sine_table):
    half_width = field.shape[-1] // 2
    lead_half = field[..., :half_width]
    tail_half = field[..., half_width:]
    return jnp.concatenate(
        [
            lead_half * cosine_table - tail_half * sine_table,
            tail_half * cosine_table + lead_half * sine_table,
        ],
        -1,
    )


def unrotate(field, cosine_table, sine_table):
    half_width = field.shape[-1] // 2
    lead_half = field[..., :half_width]
    tail_half = field[..., half_width:]
    return jnp.concatenate(
        [
            lead_half * cosine_table + tail_half * sine_table,
            tail_half * cosine_table - lead_half * sine_table,
        ],
        -1,
    )


def angles(seg_row):
    span_count = seg_row.shape[0]
    earlier = jnp.sum((seg_row[None, :] < seg_row[:, None]).astype(jnp.int32), axis=1)
    positions = jnp.arange(span_count, dtype=jnp.int32) - earlier
    frequency = rope_base ** (-jnp.arange(HD // 2, dtype=jnp.float32) * 2.0 / HD)
    phase_grid = positions.astype(jnp.float32)[:, None] * frequency[None, :]
    return (jnp.cos(phase_grid)[:, None, :], jnp.sin(phase_grid)[:, None, :])


def token_weights(seg_row, advantage_row):
    id_range = jnp.arange(RESP + 1, dtype=jnp.int32)
    onehot = (seg_row[:, None] == id_range[None, :]).astype(jnp.float32)
    counts = jnp.sum(onehot, axis=0)[:RESP]
    per_token = -advantage_row / counts
    return jnp.sum(onehot[:, :RESP] * per_token[None, :], axis=1)


def attend_back(q_rot, k_rot, v_bf, grad_context, allowed):
    score_scale = HD ** (-0.5)
    scores = (
        jnp.einsum("tkjqd,ukd->kjqtu", q_rot, k_rot, preferred_element_type=jnp.float32)
        * score_scale
    )
    scores = jnp.where(allowed, scores, masked_score)
    row_top = jnp.max(scores, axis=-1, keepdims=True)
    exponent = jnp.exp(scores - row_top)
    attention = exponent / jnp.sum(exponent, axis=-1, keepdims=True)
    attention_bf = attention.astype(jnp.bfloat16)
    grad_prob = jnp.einsum(
        "tkjqd,ukd->kjqtu", grad_context, v_bf, preferred_element_type=jnp.float32
    )
    inner_sum = jnp.sum(attention * grad_prob, axis=-1, keepdims=True)
    dscore = (attention * (grad_prob - inner_sum)).astype(jnp.bfloat16)
    grad_query = (
        jnp.einsum("kjqtu,ukd->tkjqd", dscore, k_rot, preferred_element_type=jnp.float32)
        * score_scale
    )
    grad_key = (
        jnp.einsum("kjqtu,tkjqd->ukjd", dscore, q_rot, preferred_element_type=jnp.float32)
        * score_scale
    )
    grad_value = jnp.einsum(
        "kjqtu,tkjqd->ukjd", attention_bf, grad_context, preferred_element_type=jnp.float32
    )
    return (grad_query, grad_key, grad_value)


def local(hidden, cotangent, seg_ids, advantage, w_query, w_key, w_value):
    fsdp_size = lax.axis_size("fsdp")
    share_count = max(1, fsdp_size // KVH)
    kv_local = max(1, KVH // fsdp_size)
    heads_local = H // fsdp_size
    per_copy = heads_local // kv_local
    inv_width = D ** (-0.5)

    def to_rollout(q_part, k_part, v_part):
        width_rows = q_part.shape[0]
        k_wide = jnp.repeat(k_part.reshape(width_rows, KVH, HD), share_count, axis=1).reshape(
            width_rows, KVH * share_count * HD
        )
        v_wide = jnp.repeat(v_part.reshape(width_rows, KVH, HD), share_count, axis=1).reshape(
            width_rows, KVH * share_count * HD
        )
        return (
            lax.all_to_all(q_part, "fsdp", split_axis=1, concat_axis=0, tiled=True),
            lax.all_to_all(k_wide, "fsdp", split_axis=1, concat_axis=0, tiled=True),
            lax.all_to_all(v_wide, "fsdp", split_axis=1, concat_axis=0, tiled=True),
        )

    gathered = lax.all_gather(hidden, "fsdp", axis=1, tiled=True)
    q_cols, k_cols, v_cols = to_rollout(w_query, w_key, w_value)
    token_rows = gathered[0].astype(jnp.float32)
    block_len = token_rows.shape[0]
    normed = (
        token_rows * lax.rsqrt(jnp.mean(token_rows * token_rows, axis=-1, keepdims=True) + norm_eps)
    ).astype(jnp.bfloat16)
    queries = jnp.dot(normed, q_cols, preferred_element_type=jnp.float32) * inv_width
    key_proj = jnp.dot(normed, k_cols, preferred_element_type=jnp.float32) * inv_width
    value_proj = jnp.dot(normed, v_cols, preferred_element_type=jnp.float32) * inv_width
    seg_row = seg_ids[0]
    cosine_table, sine_table = angles(seg_row)
    q_rot = rotate(queries.reshape(block_len, heads_local, HD), cosine_table, sine_table).astype(
        jnp.bfloat16
    )
    k_rot = rotate(key_proj.reshape(block_len, kv_local, HD), cosine_table, sine_table).astype(
        jnp.bfloat16
    )
    v_bf = value_proj.astype(jnp.bfloat16).reshape(block_len, kv_local, HD)
    weight_row = token_weights(seg_row, advantage[0])
    grad_context = (cotangent[0].astype(jnp.float32) * weight_row[:, None]).astype(jnp.bfloat16)
    place = jnp.arange(block_len, dtype=jnp.int32)
    allowed = (seg_row[:, None] == seg_row[None, :]) & (place[None, :] <= place[:, None])
    grad_query, grad_key, grad_value = attend_back(
        q_rot.reshape(block_len, kv_local, 1, per_copy, HD),
        k_rot,
        v_bf,
        grad_context.reshape(block_len, kv_local, 1, per_copy, HD),
        allowed,
    )
    grad_query = unrotate(grad_query.reshape(block_len, heads_local, HD), cosine_table, sine_table)
    grad_key = unrotate(grad_key.reshape(block_len, kv_local, HD), cosine_table, sine_table)
    scaled_q = (grad_query.reshape(block_len, heads_local * HD) * inv_width).astype(jnp.bfloat16)
    scaled_k = (grad_key.reshape(block_len, kv_local * HD) * inv_width).astype(jnp.bfloat16)
    scaled_v = (grad_value.reshape(block_len, kv_local * HD) * inv_width).astype(jnp.bfloat16)
    contract = (((0,), (0,)), ((), ()))
    part_q = lax.dot_general(normed, scaled_q, contract, preferred_element_type=jnp.float32).astype(
        jnp.bfloat16
    )
    part_k = lax.dot_general(normed, scaled_k, contract, preferred_element_type=jnp.float32).astype(
        jnp.bfloat16
    )
    part_v = lax.dot_general(normed, scaled_v, contract, preferred_element_type=jnp.float32).astype(
        jnp.bfloat16
    )
    back_q, back_k, back_v = (
        lax.all_to_all(part_q, "fsdp", split_axis=0, concat_axis=1, tiled=True),
        lax.all_to_all(part_k, "fsdp", split_axis=0, concat_axis=1, tiled=True),
        lax.all_to_all(part_v, "fsdp", split_axis=0, concat_axis=1, tiled=True),
    )
    width_rows = back_q.shape[0]
    sum_k = jnp.sum(
        back_k.astype(jnp.float32).reshape(width_rows, KVH, share_count, HD), axis=2
    ).reshape(width_rows, KVH * HD)
    sum_v = jnp.sum(
        back_v.astype(jnp.float32).reshape(width_rows, KVH, share_count, HD), axis=2
    ).reshape(width_rows, KVH * HD)
    query_sum = back_q.astype(jnp.float32)
    total_q, total_k, total_v = lax.psum((query_sum, sum_k, sum_v), ("section", "dp"))
    new_q = (w_query.astype(jnp.float32) - step_rate * total_q).astype(jnp.bfloat16)
    new_k = (w_key.astype(jnp.float32) - step_rate * total_k).astype(jnp.bfloat16)
    new_v = (w_value.astype(jnp.float32) - step_rate * total_v).astype(jnp.bfloat16)
    roll_q, roll_k, roll_v = to_rollout(new_q, new_k, new_v)
    return (roll_q, roll_k, roll_v)


def solution(mesh):
    in_specs = (
        P(("section", "dp"), "fsdp", None),
        P(("section", "dp"), None, "fsdp"),
        P(("section", "dp"), None),
        P(("section", "dp"), None),
        P("fsdp", None),
        P("fsdp", None),
        P("fsdp", None),
    )
    out_specs = (P(None, "fsdp"), P(None, "fsdp"), P(None, "fsdp"))
    return jax.shard_map(local, mesh=mesh, in_specs=in_specs, out_specs=out_specs, check_vma=False)
```

profile of v0, /device:TPU:9, one launch (start us, length us, event | category | flops | bytes accessed | tf_op | source)
XLA Modules:
  0.0 2327.3 jit_solution(8366162358309577115)
XLA Ops:
  11.1 5.7 all-to-all-start
  20.8 42.6 %all-to-all-done = bf16[1024,8,128]{0,2,1:T(8,128)(2,1)S(1)} async-done(((bf16[1024,8,128]{0,2,1:T(8,128)(2,1)}), bf16[1024,8,128]{0,2,1:T(8,128)(2,1)S(1)}, u32[]{:S(2)}, u32[]{:S(2)}) %all-to-all-start) | async-done | bytes 2097184 | tf_op jit(solution)/shard_map/all_to_all | solution.py:110
  63.3 5.5 all-to-all-start.2
  68.9 22.4 copy.72
  91.3 24.0 %all-to-all-done.2 = bf16[1024,8,128]{0,2,1:T(8,128)(2,1)} async-done(((bf16[1024,8,128]{0,2,1:T(8,128)(2,1)}), bf16[1024,8,128]{0,2,1:T(8,128)(2,1)}, u32[]{:S(2)}, u32[]{:S(2)}) %all-to-all-start.2) | async-done | bytes 2097184 | tf_op jit(solution)/shard_map/all_to_all | solution.py:111
  115.3 6.4 all-to-all-start.1
  133.7 393.4 %all-gather.2.cloned.1.call-done = bf16[1,512,8192]{2,1,0:T(8,128)(2,1)} async-done(((bf16[1,64,8192]{2,1,0:T(8,128)(2,1)}), bf16[1,512,8192]{2,1,0:T(8,128)(2,1)}) %all-gather.2.cloned.1.call-update) | async-done | bytes 8388624 | tf_op jit(solution)/shard_map/all_gather | solution.py:114
  536.5 46.3 %all-to-all-done.1 = bf16[1024,8,1024]{0,2,1:T(8,128)(2,1)} async-done(((bf16[1024,8,1024]{0,2,1:T(8,128)(2,1)}), bf16[1024,8,1024]{0,2,1:T(8,128)(2,1)}, u32[]{:S(2)}, u32[]{:S(2)}) %all-to-all-start.1) | async-done | bytes 16777248 | tf_op jit(solution)/shard_map/all_to_all | solution.py:109
  582.9 21.5 copy.73
  604.4 14.7 multiply_bitcast_fusion.1
  635.8 6.6 all-to-all-start.7
  642.4 13.3 fusion.3
  655.7 7.1 fusion.9
  667.6 8.1 convolution_convert_fusion.2
  675.7 12.3 all-to-all-done.7
  688.0 6.5 all-to-all-start.5
  701.3 15.5 convolution_convert_fusion
  716.9 24.1 %all-to-all-done.5 = bf16[8,1024,128]{2,1,0:T(8,128)(2,1)S(1)} async-done(((bf16[8,1024,128]{2,1,0:T(8,128)(2,1)}), bf16[8,1024,128]{2,1,0:T(8,128)(2,1)S(1)}, u32[]{:S(2)}, u32[]{:S(2)}) %all-to-all-start.5) | async-done | bytes 2097184 | tf_op jit(solution)/shard_map/all_to_all | solution.py:161
  741.0 6.4 all-to-all-start.3
  754.0 354.5 %all-to-all-done.3 = bf16[8,1024,1024]{2,1,0:T(8,128)(2,1)} async-done(((bf16[8,1024,1024]{2,1,0:T(8,128)(2,1)}), bf16[8,1024,1024]{2,1,0:T(8,128)(2,1)}, u32[]{:S(2)}, u32[]{:S(2)}) %all-to-all-start.3) | async-done | bytes 16777248 | tf_op jit(solution)/shard_map/all_to_all | solution.py:160
  1108.6 9.3 convert_bitcast_fusion
  1117.9 11.1 copy.111
  1129.0 697.3 %all-reduce.3.cloned.1.call-done = (f32[1024,8192]{1,0:T(8,128)}, f32[1024,1024]{1,0:T(8,128)}, f32[1024,1024]{1,0:T(8,128)}) async-done(((f32[1024,8192]{1,0:T(8,128)}, f32[1024,1024]{1,0:T(8,128)}, f32[1024,1024]{1,0:T(8,128)}), (f32[1024,8192]{1,0:T(8,128)}, f32[1024,1024]{1,0:T(8,128)}, f32[1024,1024]{1,0:T(8,128)})) %all-reduce.3.cloned.1.call-update) | async-done | bytes 41943056 | tf_op jit(solution)/shard_map/psum | solution.py:172
  1830.3 5.5 all-to-all-start.6
  1840.6 41.8 %all-to-all-done.6 = bf16[1024,8,128]{2,0,1:T(8,128)(2,1)S(1)} async-done(((bf16[1024,8,128]{2,0,1:T(8,128)(2,1)}), bf16[1024,8,128]{2,0,1:T(8,128)(2,1)S(1)}, u32[]{:S(2)}, u32[]{:S(2)}) %all-to-all-start.6) | async-done | bytes 2097184 | tf_op jit(solution)/shard_map/all_to_all | solution.py:110
  1882.4 5.5 all-to-all-start.8
  1887.9 16.2 subtract_convert_fusion
  1904.0 6.9 copy.129
  1910.9 23.4 %all-to-all-done.8 = bf16[1024,8,128]{2,0,1:T(8,128)(2,1)} async-done(((bf16[1024,8,128]{2,0,1:T(8,128)(2,1)}), bf16[1024,8,128]{2,0,1:T(8,128)(2,1)}, u32[]{:S(2)}, u32[]{:S(2)}) %all-to-all-start.8) | async-done | bytes 2097184 | tf_op jit(solution)/shard_map/all_to_all | solution.py:111
  1934.3 6.3 all-to-all-start.4
  1940.6 361.5 %all-to-all-done.4 = bf16[1024,8,1024]{2,0,1:T(8,128)(2,1)} async-done(((bf16[1024,8,1024]{2,0,1:T(8,128)(2,1)}), bf16[1024,8,1024]{2,0,1:T(8,128)(2,1)}, u32[]{:S(2)}, u32[]{:S(2)}) %all-to-all-start.4) | async-done | bytes 16777248 | tf_op jit(solution)/shard_map/all_to_all | solution.py:109
  2302.0 13.9 copy.136
  (66 shorter events, 77.4 us)
Async XLA Ops:
  11.1 52.2 %all-to-all-start = ((bf16[1024,8,128]{0,2,1:T(8,128)(2,1)}), bf16[1024,8,128]{0,2,1:T(8,128)(2,1)S(1)}, u32[]{:S(2)}, u32[]{:S(2)}) async-start(bf16[1024,8,128]{0,2,1:T(8,128)(2,1)} %bitcast.199), calls=%async_computation | async-start | bytes 4194304 | tf_op jit(solution)/shard_map/all_to_all | solution.py:110
  63.3 51.9 %all-to-all-start.2 = ((bf16[1024,8,128]{0,2,1:T(8,128)(2,1)}), bf16[1024,8,128]{0,2,1:T(8,128)(2,1)}, u32[]{:S(2)}, u32[]{:S(2)}) async-start(bf16[1024,8,128]{0,2,1:T(8,128)(2,1)} %bitcast.198), calls=%async_computation.2 | async-start | bytes 4194304 | tf_op jit(solution)/shard_map/all_to_all | solution.py:111
  115.3 7.1 copy-start.4
  115.3 467.6 %all-to-all-start.1 = ((bf16[1024,8,1024]{0,2,1:T(8,128)(2,1)}), bf16[1024,8,1024]{0,2,1:T(8,128)(2,1)}, u32[]{:S(2)}, u32[]{:S(2)}) async-start(bf16[1024,8,1024]{0,2,1:T(8,128)(2,1)} %bitcast.188), calls=%async_computation.1 | async-start | bytes 33554432 | tf_op jit(solution)/shard_map/all_to_all | solution.py:109
  121.7 2.4 copy-start.7
  121.7 2.5 copy-start.8
  121.7 405.4 %all-gather.2.cloned.1.call-start = ((), (), s32[]{:S(2)}) async-start(), calls=%async_computation.9 | async-start | bytes 9437184 | tf_op jit(solution)/shard_map/all_gather | solution.py:114
  129.7 402.7 %copy-start.6 = (bf16[8,1024,128]{2,1,0:T(8,128)(2,1)S(1)}, bf16[8,1024,128]{2,1,0:T(8,128)(2,1)}, u32[]{:S(2)}) copy-start(bf16[8,1024,128]{2,1,0:T(8,128)(2,1)} %copy.71) | copy-start | bytes 6291460
  527.1 5.8 copy-start.2
  623.3 4.3 copy-start
  623.3 4.2 copy-start.5
  623.4 6.9 slice-start
  627.6 3.0 slice-start.1
  635.8 52.2 %all-to-all-start.7 = ((bf16[8,1024,128]{2,1,0:T(8,128)(2,1)}), bf16[8,1024,128]{2,1,0:T(8,128)(2,1)}, u32[]{:S(2)}, u32[]{:S(2)}) async-start(bf16[8,1024,128]{2,1,0:T(8,128)(2,1)} %bitcast.202), calls=%async_computation.7 | async-start | bytes 4194304 | tf_op jit(solution)/shard_map/all_to_all | solution.py:162
  662.8 2.0 copy-start.1
  688.0 53.0 %all-to-all-start.5 = ((bf16[8,1024,128]{2,1,0:T(8,128)(2,1)}), bf16[8,1024,128]{2,1,0:T(8,128)(2,1)S(1)}, u32[]{:S(2)}, u32[]{:S(2)}) async-start(bf16[8,1024,128]{2,1,0:T(8,128)(2,1)} %bitcast.203), calls=%async_computation.5 | async-start | bytes 4194304 | tf_op jit(solution)/shard_map/all_to_all | solution.py:161
  741.0 367.6 %all-to-all-start.3 = ((bf16[8,1024,1024]{2,1,0:T(8,128)(2,1)}), bf16[8,1024,1024]{2,1,0:T(8,128)(2,1)}, u32[]{:S(2)}, u32[]{:S(2)}) async-start(bf16[8,1024,1024]{2,1,0:T(8,128)(2,1)} %bitcast.192), calls=%async_computation.3 | async-start | bytes 33554432 | tf_op jit(solution)/shard_map/all_to_all | solution.py:160
  747.4 1078.9 %all-reduce.3.cloned.1.call-start = ((), (), s32[]{:S(2)}) async-start(), calls=%async_computation.10 | async-start | bytes 83886080 | tf_op jit(solution)/shard_map/psum | solution.py:172
  1129.0 697.3 %copy-start.3 = (bf16[1024,1024]{1,0:T(8,128)(2,1)S(1)}, bf16[1024,1024]{1,0:T(8,128)(2,1)}, u32[]{:S(2)}) copy-start(bf16[1024,1024]{1,0:T(8,128)(2,1)} %param.12) | copy-start | bytes 6291460
  1830.3 52.0 %all-to-all-start.6 = ((bf16[1024,8,128]{2,0,1:T(8,128)(2,1)}), bf16[1024,8,128]{2,0,1:T(8,128)(2,1)S(1)}, u32[]{:S(2)}, u32[]{:S(2)}) async-start(bf16[1024,8,128]{2,0,1:T(8,128)(2,1)} %copy_bitcast_fusion.4), calls=%async_computation.6 | async-start | bytes 4194304 | tf_op jit(solution)/shard_map/all_to_all | solution.py:110
  1882.4 52.0 %all-to-all-start.8 = ((bf16[1024,8,128]{2,0,1:T(8,128)(2,1)}), bf16[1024,8,128]{2,0,1:T(8,128)(2,1)}, u32[]{:S(2)}, u32[]{:S(2)}) async-start(bf16[1024,8,128]{2,0,1:T(8,128)(2,1)} %copy_bitcast_fusion.3), calls=%async_computation.8 | async-start | bytes 4194304 | tf_op jit(solution)/shard_map/all_to_all | solution.py:111
  1934.3 367.7 %all-to-all-start.4 = ((bf16[1024,8,1024]{2,0,1:T(8,128)(2,1)}), bf16[1024,8,1024]{2,0,1:T(8,128)(2,1)}, u32[]{:S(2)}, u32[]{:S(2)}) async-start(bf16[1024,8,1024]{2,0,1:T(8,128)(2,1)} %bitcast.189), calls=%async_computation.4 | async-start | bytes 33554432 | tf_op jit(solution)/shard_map/all_to_all | solution.py:109
Sparse Core Ops, SparseCore 0:
  124.6 402.4 all-gather.1
  1129.1 697.1 all-reduce.2
where the time goes:
time: 2340 us; the launch traced here: 2330 us
  waiting for transfers between devices  2020 us (86%)
  local copies, waits for them, and re-layouts  105 us (4%)
  matrix products  71.1 us (3%)
  other arithmetic  60.4 us (3%)
  starting transfers between devices  54.4 us (2%)
    psum x1, waiting for transfers between devices, local(): lax.psum((query_sum, sum_k, sum_v), ('section', 'dp'))  697 us
    all_to_all x2, waiting for transfers between devices, to_rollout(): lax.all_to_all(q_part, 'fsdp', split_axis=1, concat_axis=0, tiled=True)  408 us
    all_gather x1, waiting for transfers between devices, local(): gathered = lax.all_gather(hidden, 'fsdp', axis=1, tiled=True)  393 us
    all_to_all x1, waiting for transfers between devices, local(): lax.all_to_all(part_q, 'fsdp', split_axis=0, concat_axis=1, tiled=True)  355 us
    all_to_all x2, waiting for transfers between devices, to_rollout(): lax.all_to_all(k_wide, 'fsdp', split_axis=1, concat_axis=0, tiled=True)  84.4 us
    unnamed x30, local copies, waits for them, and re-layouts  55.6 us
    all_to_all x2, waiting for transfers between devices, to_rollout(): lax.all_to_all(v_wide, 'fsdp', split_axis=1, concat_axis=0, tiled=True)  47.4 us
  transfers between devices with their start and end apart: 11, of which 11 were waited for; matrix products, arithmetic and copies ran while one was open for 6% of the time, Pallas kernels for 0%

commit v1 on v0

--- a/solution.py
+++ b/solution.py
@@ -1,6 +1,10 @@
+import functools
+
 import jax
 import jax.numpy as jnp
 from jax import lax
+from jax.experimental import pallas as pl
+from jax.experimental.pallas import tpu as pltpu
 from jax.sharding import PartitionSpec as P
 
 D = 8192
@@ -88,6 +92,247 @@
     )
     return (grad_query, grad_key, grad_value)
 
+MESH = pl.DeviceIdType.MESH
+
+
+def remote(src, dst, send, recv, device):
+    return pltpu.make_async_remote_copy(
+        src_ref=src, dst_ref=dst, send_sem=send, recv_sem=recv, device_id=device, device_id_type=MESH
+    )
+
+
+def gather_kernel(
+    count, share, n_ref, wq_ref, wkv_ref, hid_ref, qc_ref, kv_ref,
+    w_send, w_recv, z_send, z_recv, y_send, y_recv, x_send, x_recv, g_send, g_recv, c_send, c_recv,
+    own_sem,
+):
+    s, f, d = lax.axis_index("section"), lax.axis_index("fsdp"), lax.axis_index("dp")
+    line = count // 2
+    a, b = f // 2, f % 2
+    to_y, to_x, to_c = {"fsdp": a * 2 + 1 - b}, {"section": 1 - s}, {"dp": 1 - d}
+    rows = wq_ref.shape[0]
+    part = rows // 4
+    mine, across = s * 2 + d, (1 - s) * 2 + d
+    pairs = ((wq_ref, qc_ref), (wkv_ref, kv_ref))
+    via_x = line // 4
+
+    barrier = pltpu.get_barrier_semaphore()
+
+    def greet(k, carry):
+        pl.semaphore_signal(barrier, inc=1, device_id={"fsdp": (f + k) % count}, device_id_type=MESH)
+        return carry
+
+    lax.fori_loop(1, count, greet, 0)
+    pl.semaphore_signal(barrier, inc=1, device_id=to_x, device_id_type=MESH)
+    pl.semaphore_signal(barrier, inc=1, device_id=to_c, device_id_type=MESH)
+    pl.semaphore_wait(barrier, count + 1)
+
+    def columns(i, target):
+        wide = pairs[i][1].shape[1]
+        at = target if i == 0 else target // share
+        return pl.ds(pl.multiple_of(at * wide, 128), wide)
+
+    def piece(i, shard, quarter):
+        return pairs[i][1].at[pl.ds(pl.multiple_of(shard * rows + quarter * part, 16), part)]
+
+    def w_copy(i, stage, k, src, dst, device):
+        return remote(src, dst, w_send.at[stage, i, k], w_recv.at[stage, i, k], device)
+
+    def own_row(j):
+        return ((a + line - j) % line) * 2 + b
+
+    def other_row(j):
+        return ((a + line - j) % line) * 2 + 1 - b
+
+    def h_copy(sems, j, src, dst, device):
+        return remote(src, dst, sems[0].at[j], sems[1].at[j], device)
+
+    zs, ys, xs, gs = (z_send, z_recv), (y_send, y_recv), (x_send, x_recv), (g_send, g_recv)
+
+    def core(kind, j, src, dst):
+        return remote(src, dst, c_send.at[kind, j], c_recv.at[kind, j], to_c)
+
+    def z_first(j, carry):
+        target = ((a + j) % line) * 2 + b
+        h_copy(zs, j, n_ref, hid_ref.at[0, f], {"fsdp": target}).start()
+        return carry
+
+    h_copy(ys, 0, n_ref, hid_ref.at[0, f], to_y).start()
+    h_copy(xs, 0, n_ref, hid_ref.at[2, f], to_x).start()
+    core(0, 0, n_ref, hid_ref.at[1, f]).start()
+    lax.fori_loop(1, line, z_first, 0)
+
+    def w_first(k, carry):
+        target = (f + k) % count
+        for i in range(2):
+            src = pairs[i][0].at[pl.ds(pl.multiple_of(mine * part, 16), part), columns(i, target)]
+            w_copy(i, 0, k, src, piece(i, f, mine), {"fsdp": target}).start()
+        return carry
+
+    lax.fori_loop(1, count, w_first, 0)
+    locals_ = [pltpu.make_async_copy(n_ref, hid_ref.at[0, f], own_sem.at[0])]
+    for i in range(2):
+        dst = pairs[i][1].at[pl.ds(pl.multiple_of(f * rows, 16), rows)]
+        locals_.append(pltpu.make_async_copy(pairs[i][0].at[:, columns(i, f)], dst, own_sem.at[1 + i]))
+    for copy in locals_:
+        copy.start()
+
+    def z_next(j, carry):
+        at = hid_ref.at[0, own_row(j)]
+        h_copy(zs, j, at, at, to_y).wait_recv()
+        h_copy(ys, j, at, at, to_y).start()
+        h_copy(xs, j, at, hid_ref.at[2, own_row(j)], to_x).start()
+        core(0, j, at, hid_ref.at[1, own_row(j)]).start()
+        return carry
+
+    lax.fori_loop(1, line, z_next, 0)
+
+    def w_next(k, carry):
+        for i in range(2):
+            at = piece(i, (f + count - k) % count, mine)
+            w_copy(i, 0, k, at, at, to_x).wait_recv()
+            w_copy(i, 1, k, at, at, to_x).start()
+            w_copy(i, 2, k, at, at, to_c).start()
+        return carry
+
+    def y_next(j, via):
+        at = hid_ref.at[0, other_row(j)]
+        h_copy(ys, j, at, at, to_y).wait_recv()
+        core(1, j, at, hid_ref.at[1, other_row(j)]).start()
+        if via:
+            h_copy(gs, j, at, hid_ref.at[2, other_row(j)], to_x).start()
+
+    def x_next(j, via):
+        at = hid_ref.at[2, own_row(j)]
+        h_copy(xs, j, at, at, to_x).wait_recv()
+        core(2, j, at, hid_ref.at[3, own_row(j)]).start()
+        if not via:
+            h_copy(gs, j, at, at, to_y).start()
+
+    def both(via, j, carry):
+        y_next(j, via)
+        x_next(j, via)
+        return carry
+
+    half = (count + 1) // 2
+    lax.fori_loop(1, half, w_next, 0)
+    lax.fori_loop(0, via_x, functools.partial(both, True), 0)
+    lax.fori_loop(via_x, line, functools.partial(both, False), 0)
+    lax.fori_loop(half, count, w_next, 0)
+
+    def w_last(k, carry):
+        for i in range(2):
+            at = piece(i, (f + count - k) % count, across)
+            w_copy(i, 1, k, at, at, to_x).wait_recv()
+            w_copy(i, 3, k, at, at, to_c).start()
+        return carry
+
+    lax.fori_loop(1, count, w_last, 0)
+
+    def g_last(j, carry):
+        at = hid_ref.at[2, other_row(j)]
+        h_copy(gs, j, at, at, to_x).wait_recv()
+        core(3, j, at, hid_ref.at[3, other_row(j)]).start()
+        return carry
+
+    lax.fori_loop(0, line, g_last, 0)
+
+    def w_end(k, carry):
+        shard = (f + count - k) % count
+        for i in range(2):
+            near, far = piece(i, shard, s * 2 + 1 - d), piece(i, shard, (1 - s) * 2 + 1 - d)
+            w_copy(i, 2, k, near, near, to_c).wait_recv()
+            w_copy(i, 3, k, far, far, to_c).wait_recv()
+            for stage in range(4):
+                w_copy(i, stage, k, near, near, to_c).wait_send()
+        return carry
+
+    lax.fori_loop(1, count, w_end, 0)
+
+    def h_end(j, carry):
+        for kind, block, place in ((0, 1, own_row(j)), (1, 1, other_row(j)), (2, 3, own_row(j)), (3, 3, other_row(j))):
+            at = hid_ref.at[block, place]
+            core(kind, j, at, at).wait_recv()
+            core(kind, j, at, at).wait_send()
+        for sems in (ys, xs, gs):
+            h_copy(sems, j, n_ref, n_ref, to_y).wait_send()
+        return carry
+
+    lax.fori_loop(0, line, h_end, 0)
+
+    def z_end(j, carry):
+        h_copy(zs, j, n_ref, n_ref, to_y).wait_send()
+        return carry
+
+    lax.fori_loop(1, line, z_end, 0)
+    for copy in locals_:
+        copy.wait()
+
+
+def gather_all(count, share, normed, w_query, wkv):
+    line = count // 2
+    rows, width = normed.shape
+    dma = pltpu.SemaphoreType.DMA
+    pair = lambda *shape: [dma(shape), dma(shape)]
+    out = lambda *shape: jax.ShapeDtypeStruct(shape, jnp.bfloat16)
+    kv_wide = wkv.shape[1] // min(count, KVH)
+    return pl.pallas_call(
+        functools.partial(gather_kernel, count, share),
+        out_shape=(
+            out(4, count, rows, width),
+            out(count * w_query.shape[0], w_query.shape[1] // count),
+            out(count * wkv.shape[0], kv_wide),
+        ),
+        in_specs=[pl.BlockSpec(memory_space=pl.ANY)] * 3,
+        out_specs=[pl.BlockSpec(memory_space=pl.ANY)] * 3,
+        scratch_shapes=pair(4, 2, count) + pair(line) * 4 + pair(4, line) + [dma((3,))],
+        compiler_params=pltpu.CompilerParams(collective_id=0, has_side_effects=True),
+        name="gather_all",
+    )(normed, w_query, wkv)
+
+
+def exchange_kernel(q_ref, kv_ref, q_all, kv_all, send, recv, own_sem):
+    s, d = lax.axis_index("section"), lax.axis_index("dp")
+    to_x, to_c = {"section": 1 - s}, {"dp": 1 - d}
+    barrier = pltpu.get_barrier_semaphore()
+    pl.semaphore_signal(barrier, inc=1, device_id=to_x, device_id_type=MESH)
+    pl.semaphore_signal(barrier, inc=1, device_id=to_c, device_id_type=MESH)
+    pl.semaphore_wait(barrier, 2)
+    pairs = ((q_ref, q_all), (kv_ref, kv_all))
+    waits = []
+    for i, (src, dst) in enumerate(pairs):
+        over = remote(src, dst.at[2], send.at[i, 0], recv.at[i, 0], to_x)
+        near = remote(src, dst.at[1], send.at[i, 1], recv.at[i, 1], to_c)
+        own = pltpu.make_async_copy(src, dst.at[0], own_sem.at[i])
+        for copy in (over, near, own):
+            copy.start()
+        waits.append((over, near, own))
+    lasts = []
+    for i, (src, dst) in enumerate(pairs):
+        waits[i][0].wait_recv()
+        last = remote(dst.at[2], dst.at[3], send.at[i, 2], recv.at[i, 2], to_c)
+        last.start()
+        lasts.append(last)
+    for i in range(2):
+        waits[i][0].wait_send()
+        waits[i][1].wait()
+        waits[i][2].wait()
+        lasts[i].wait()
+
+
+def exchange(scaled_q, scaled_kv):
+    dma = pltpu.SemaphoreType.DMA
+    out = lambda x: jax.ShapeDtypeStruct((4,) + x.shape, jnp.bfloat16)
+    return pl.pallas_call(
+        exchange_kernel,
+        out_shape=(out(scaled_q), out(scaled_kv)),
+        in_specs=[pl.BlockSpec(memory_space=pl.ANY)] * 2,
+        out_specs=[pl.BlockSpec(memory_space=pl.ANY)] * 2,
+        scratch_shapes=[dma((2, 3)), dma((2, 3)), dma((2,))],
+        compiler_params=pltpu.CompilerParams(collective_id=1, has_side_effects=True),
+        name="exchange",
+    )(scaled_q, scaled_kv)
+
 
 def local(hidden, cotangent, seg_ids, advantage, w_query, w_key, w_value):
     fsdp_size = lax.axis_size("fsdp")
@@ -97,30 +342,26 @@
     per_copy = heads_local // kv_local
     inv_width = D ** (-0.5)
 
-    def to_rollout(q_part, k_part, v_part):
-        width_rows = q_part.shape[0]
-        k_wide = jnp.repeat(k_part.reshape(width_rows, KVH, HD), share_count, axis=1).reshape(
-            width_rows, KVH * share_count * HD
-        )
-        v_wide = jnp.repeat(v_part.reshape(width_rows, KVH, HD), share_count, axis=1).reshape(
-            width_rows, KVH * share_count * HD
-        )
-        return (
-            lax.all_to_all(q_part, "fsdp", split_axis=1, concat_axis=0, tiled=True),
-            lax.all_to_all(k_wide, "fsdp", split_axis=1, concat_axis=0, tiled=True),
-            lax.all_to_all(v_wide, "fsdp", split_axis=1, concat_axis=0, tiled=True),
-        )
-
-    gathered = lax.all_gather(hidden, "fsdp", axis=1, tiled=True)
-    q_cols, k_cols, v_cols = to_rollout(w_query, w_key, w_value)
-    token_rows = gathered[0].astype(jnp.float32)
-    block_len = token_rows.shape[0]
-    normed = (
-        token_rows * lax.rsqrt(jnp.mean(token_rows * token_rows, axis=-1, keepdims=True) + norm_eps)
+    rows = hidden[0].astype(jnp.float32)
+    own_normed = (
+        rows * lax.rsqrt(jnp.mean(rows * rows, axis=-1, keepdims=True) + norm_eps)
     ).astype(jnp.bfloat16)
+    width_rows = w_key.shape[0]
+    groups = KVH // kv_local
+    wkv = jnp.concatenate(
+        [
+            w_key.reshape(width_rows, groups, kv_local * HD),
+            w_value.reshape(width_rows, groups, kv_local * HD),
+        ],
+        axis=2,
+    ).reshape(width_rows, 2 * KVH * HD)
+    normed_all, q_cols, kv_cols = gather_all(fsdp_size, share_count, own_normed, w_query, wkv)
+    normed_all = normed_all.reshape(4, -1, D)
+    normed = normed_all[0]
+    block_len = normed.shape[0]
     queries = jnp.dot(normed, q_cols, preferred_element_type=jnp.float32) * inv_width
-    key_proj = jnp.dot(normed, k_cols, preferred_element_type=jnp.float32) * inv_width
-    value_proj = jnp.dot(normed, v_cols, preferred_element_type=jnp.float32) * inv_width
+    kv_proj = jnp.dot(normed, kv_cols, preferred_element_type=jnp.float32) * inv_width
+    key_proj, value_proj = kv_proj[:, : kv_local * HD], kv_proj[:, kv_local * HD :]
     seg_row = seg_ids[0]
     cosine_table, sine_table = angles(seg_row)
     q_rot = rotate(queries.reshape(block_len, heads_local, HD), cosine_table, sine_table).astype(
@@ -146,35 +387,13 @@
     scaled_q = (grad_query.reshape(block_len, heads_local * HD) * inv_width).astype(jnp.bfloat16)
     scaled_k = (grad_key.reshape(block_len, kv_local * HD) * inv_width).astype(jnp.bfloat16)
     scaled_v = (grad_value.reshape(block_len, kv_local * HD) * inv_width).astype(jnp.bfloat16)
-    contract = (((0,), (0,)), ((), ()))
-    part_q = lax.dot_general(normed, scaled_q, contract, preferred_element_type=jnp.float32).astype(
-        jnp.bfloat16
-    )
-    part_k = lax.dot_general(normed, scaled_k, contract, preferred_element_type=jnp.float32).astype(
-        jnp.bfloat16
-    )
-    part_v = lax.dot_general(normed, scaled_v, contract, preferred_element_type=jnp.float32).astype(
-        jnp.bfloat16
-    )
-    back_q, back_k, back_v = (
-        lax.all_to_all(part_q, "fsdp", split_axis=0, concat_axis=1, tiled=True),
-        lax.all_to_all(part_k, "fsdp", split_axis=0, concat_axis=1, tiled=True),
-        lax.all_to_all(part_v, "fsdp", split_axis=0, concat_axis=1, tiled=True),
-    )
-    width_rows = back_q.shape[0]
-    sum_k = jnp.sum(
-        back_k.astype(jnp.float32).reshape(width_rows, KVH, share_count, HD), axis=2
-    ).reshape(width_rows, KVH * HD)
-    sum_v = jnp.sum(
-        back_v.astype(jnp.float32).reshape(width_rows, KVH, share_count, HD), axis=2
-    ).reshape(width_rows, KVH * HD)
-    query_sum = back_q.astype(jnp.float32)
-    total_q, total_k, total_v = lax.psum((query_sum, sum_k, sum_v), ("section", "dp"))
-    new_q = (w_query.astype(jnp.float32) - step_rate * total_q).astype(jnp.bfloat16)
-    new_k = (w_key.astype(jnp.float32) - step_rate * total_k).astype(jnp.bfloat16)
-    new_v = (w_value.astype(jnp.float32) - step_rate * total_v).astype(jnp.bfloat16)
-    roll_q, roll_k, roll_v = to_rollout(new_q, new_k, new_v)
-    return (roll_q, roll_k, roll_v)
+    all_q, all_kv = exchange(scaled_q, jnp.concatenate([scaled_k, scaled_v], axis=1))
+    contract = (((0, 1), (0, 1)), ((), ()))
+    total_q = lax.dot_general(normed_all, all_q, contract, preferred_element_type=jnp.float32)
+    total_kv = lax.dot_general(normed_all, all_kv, contract, preferred_element_type=jnp.float32)
+    new_q = (q_cols.astype(jnp.float32) - step_rate * total_q).astype(jnp.bfloat16)
+    new_kv = (kv_cols.astype(jnp.float32) - step_rate * total_kv).astype(jnp.bfloat16)
+    return (new_q, new_kv[:, : kv_local * HD], new_kv[:, kv_local * HD :])
 
 
 def solution(mesh):

time: 2340 us -> 489 us (0.21)
  waiting for transfers between devices: 2020 us -> 0 us
  Pallas kernels: 0 us -> 348 us
  local copies, waits for them, and re-layouts: 105 us -> 25 us
  starting transfers between devices: 54.4 us -> 0 us
  other arithmetic: 60.4 us -> 16.1 us
    all_to_all x9 -> x0, waiting for transfers between devices: 930 us -> none  [the longest x2 408 us: to_rollout(): lax.all_to_all(q_part, 'fsdp', split_axis=1, concat_axis=0, tiled=True)]
    psum x1 -> x0, waiting for transfers between devices: 697 us -> none  [local(): lax.psum((query_sum, sum_k, sum_v), ('section', 'dp'))]
    all_gather x1 -> x0, waiting for transfers between devices: 393 us -> none  [local(): gathered = lax.all_gather(hidden, 'fsdp', axis=1, tiled=True)]
    pallas_call x0 -> x2, Pallas kernels: none -> 348 us  [the longest x1 307 us: gather_all(): pl.pallas_call(functools.partial(gather_kernel, count, share), out_shape=...]
    all_to_all x9 -> x0, starting transfers between devices: 54.4 us -> none  [the longest x2 12.6 us: to_rollout(): lax.all_to_all(q_part, 'fsdp', split_axis=1, concat_axis=0, tiled=True)]
    unnamed x30 -> x27, local copies, waits for them, and re-layouts: 55.6 us -> 12.4 us
    all_to_all x4 -> x0, local copies, waits for them, and re-layouts: 34.8 us -> none  [the longest x2 28.4 us: to_rollout(): lax.all_to_all(q_part, 'fsdp', split_axis=1, concat_axis=0, tiled=True)]
    dot_general x4 -> x3, matrix products: 32 us -> 64.8 us  [the longest x1 45.1 us: local(): lax.dot_general(normed_all, all_q, contract, preferred_element_type=jnp.f...]
  transfers between devices with their start and end apart: 11 -> 0, of which waited for: 11 -> 0; matrix products, arithmetic and copies ran while one was open for 6% -> 0% of each run, Pallas kernels for 0% -> 0%
where the time goes in v1:
time: 489 us; the launch traced here: 485 us
  Pallas kernels  348 us (71%)
  matrix products  94.2 us (19%)
  local copies, waits for them, and re-layouts  25 us (5%)
  other arithmetic  16.1 us (3%)
    pallas_call x1, Pallas kernels, gather_all(): pl.pallas_call(functools.partial(gather_kernel, count, share), out_shape=...  307 us
    dot_general x1, matrix products, local(): lax.dot_general(normed_all, all_q, contract, preferred_element_type=jnp.f...  45.1 us
    pallas_call x1, Pallas kernels, exchange(): pl.pallas_call(exchange_kernel, out_shape=(out(scaled_q), out(scaled_kv))...  41.2 us
    dot_general x1, matrix products, local(): lax.dot_general(normed_all, all_kv, contract, preferred_element_type=jnp....  17.3 us
    dot_general x1, matrix products, local(): jnp.dot(normed, q_cols, preferred_element_type=jnp.float32) * inv_width  14.3 us
    unnamed x27, local copies, waits for them, and re-layouts  12.4 us

profile of v1, /device:TPU:9, one launch (start us, length us, event | category | flops | bytes accessed | tf_op | source)
XLA Modules:
  0.0 485.1 jit_solution(15721757045796132093)
XLA Ops:
  0.6 1.0 convert_reduce_fusion
  1.7 1.0 multiply_cosine_fusion
  2.7 2.2 copy.60
  6.0 3.5 copy.62
  9.8 1.2 fusion.17.n_ref
  11.1 307.2 %gather_all.1 = (bf16[4,8,64,8192]{3,2,1,0:T(8,128)(2,1)}, bf16[8192,1024]{1,0:T(8,128)(2,1)}, bf16[8192,256]{1,0:T(8,128)(2,1)}) custom-call(bf16[64,8192]{1,0:T(8,128)(2,1)} %fusion.17.n_ref, bf16[1024,8192]{1,0:T(8,128)(2,1)} %wq_ref.1, bf16[1024,2048]{1,0:T(8,128)(2,1)} %bitcast.157), custom_call_target="tpu_custom_call" | custom-call | tf_op jit(solution)/shard_map/gather_all/pallas_call | solution.py:279
  318.3 7.8 %slice.47 = bf16[1,8,64,8192]{3,2,1,0:T(8,128)(2,1)} slice(bf16[4,8,64,8192]{3,2,1,0:T(8,128)(2,1)} %get-tuple-element.9), slice={[0:1], [0:8], [0:64], [0:8192]} | slice | bytes 16777216 | tf_op jit(solution)/shard_map/slice | solution.py:360
  326.1 14.3 %multiply_bitcast_fusion.1 = f32[64,8,8,128]{3,1,2,0:T(8,128)S(1)} fusion(bf16[512,8192]{1,0:T(8,128)(2,1)} %bitcast.158, bf16[8192,1024]{1,0:T(8,128)(2,1)} %get-tuple-element.8), kind=kOutput, calls=%fused_computation.35 | convolution fusion | flops 8590458880 | bytes 27262976 | tf_op jit(solution)/shard_map/dot_general | solution.py:362
  340.9 0.7 fusion.69
  341.6 0.8 subtract_convert_fusion
  342.4 0.7 slice-done
  343.0 1.3 slice-done.1
  344.3 1.4 copy-done.7
  345.7 2.4 convolution_multiply_fusion
  348.1 1.4 fusion.59
  349.7 2.3 fusion.10
  352.1 1.8 fusion.9
  354.6 3.2 fusion.5
  357.8 2.7 fusion.11
  360.6 2.0 copy-done.1
  362.5 1.3 fusion.23
  363.9 1.2 fusion.51
  365.2 1.8 copy.55
  367.1 6.4 %fusion.30 = bf16[512,128]{1,0:T(8,128)(2,1)S(1)} fusion(f32[8,512]{1,0:T(8,128)S(1)} %fusion.9, f32[8,512]{1,0:T(8,128)S(1)} %get-tuple-element.27, f32[512,512,8]{1,0,2:T(8,128)} %copy-done, pred[512,512]{0,1:T(8,128)(4,1)S(1)} %fusion.38, f32[512,8,128]{0,2,1:T(8,128)} %bitcast.164, f32[512]{0:T(512)S(1)} %fusion.61), kind=kOutput, calls=%fused_computation.43 | convolution fusion | flops 548536320 | bytes 10913792 | tf_op jit(solution)/shard_map/kjqtu,tkjqd->ukjd/dot_general | solution.py:90
  373.5 0.7 pad_maximum_fusion.2.kv_ref
  374.2 1.9 multiply_bitcast_fusion
  376.1 1.0 multiply_add_fusion
  377.2 1.6 copy_bitcast_fusion.q_ref
  378.7 41.2 %exchange.1 = (bf16[4,512,1024]{2,1,0:T(8,128)(2,1)}, bf16[4,512,256]{2,1,0:T(8,128)(2,1)}) custom-call(bf16[512,1024]{1,0:T(8,128)(2,1)} %copy_bitcast_fusion.q_ref, bf16[512,256]{1,0:T(8,128)(2,1)} %pad_maximum_fusion.2.kv_ref), custom_call_target="tpu_custom_call" | custom-call | tf_op jit(solution)/shard_map/exchange/pallas_call | solution.py:326
  419.9 17.3 %fusion.4 = bf16[8192,256]{1,0:T(8,128)(2,1)S(1)} fusion(bf16[4,512,8192]{2,1,0:T(8,128)(2,1)} %bitcast.165, bf16[4,512,256]{2,1,0:T(8,128)(2,1)} %get-tuple-element.12, bf16[8192,256]{1,0:T(8,128)(2,1)} %get-tuple-element.10), kind=kOutput, calls=%fused_computation.6 | convolution fusion | flops 8598323200 | bytes 42991616 | tf_op jit(solution)/shard_map/dot_general | solution.py:393
  437.3 2.3 fusion.68
  439.6 45.1 %fusion.1 = bf16[8192,1024]{1,0:T(8,128)(2,1)} fusion(bf16[8192,1024]{1,0:T(8,128)(2,1)} %get-tuple-element.8, bf16[4,512,8192]{2,1,0:T(8,128)(2,1)} %bitcast.166, bf16[4,512,1024]{2,1,0:T(8,128)(2,1)} %get-tuple-element.11), kind=kOutput, calls=%fused_computation.2 | convolution fusion | flops 34393292800 | bytes 71303168 | tf_op jit(solution)/shard_map/dot_general | solution.py:392
  (35 shorter events, 3.1 us)
Async XLA Ops:
  0.6 4.3 copy-start.5
  6.0 3.5 copy-start.4
  340.8 2.2 slice-start
  340.9 3.5 slice-start.1
  341.5 4.1 copy-start.7
  345.7 3.8 copy-start.6
  352.0 5.8 %copy-start = (f32[512,512,8]{1,0,2:T(8,128)}, f32[512,512,8]{1,0,2:T(8,128)S(1)}, u32[]{:S(2)}) copy-start(f32[512,512,8]{1,0,2:T(8,128)S(1)} %get-tuple-element.28) | copy-start | bytes 25165828
  352.0 1.9 copy-start.8
  352.1 2.0 copy-start.3
  360.6 2.0 copy-start.1
  367.1 7.1 %copy-start.2 = (bf16[8,512,512]{1,2,0:T(8,128)(2,1)S(1)}, bf16[8,512,512]{1,2,0:T(8,128)(2,1)}, u32[]{:S(2)}) copy-start(bf16[8,512,512]{1,2,0:T(8,128)(2,1)} %copy-done.1) | copy-start | bytes 12582916

commit v2 on v1

--- a/solution.py
+++ b/solution.py
@@ -212,13 +212,16 @@
     def both(via, j, carry):
         y_next(j, via)
         x_next(j, via)
-        return carry
-
-    half = (count + 1) // 2
-    lax.fori_loop(1, half, w_next, 0)
+        w_next(2 * j + 1, 0)
+
+        @pl.when(2 * j + 2 < count)
+        def _():
+            w_next(2 * j + 2, 0)
+
+        return carry
+
     lax.fori_loop(0, via_x, functools.partial(both, True), 0)
     lax.fori_loop(via_x, line, functools.partial(both, False), 0)
-    lax.fori_loop(half, count, w_next, 0)
 
     def w_last(k, carry):
         for i in range(2):
@@ -289,6 +292,42 @@
         compiler_params=pltpu.CompilerParams(collective_id=0, has_side_effects=True),
         name="gather_all",
     )(normed, w_query, wkv)
+
+
+def project_kernel(n_ref, wq_ref, wkv_ref, q_ref, kv_ref):
+    @pl.when(pl.program_id(0) == 0)
+    def _():
+        q_ref[...] = jnp.zeros_like(q_ref)
+        kv_ref[...] = jnp.zeros_like(kv_ref)
+
+    normed = n_ref[0]
+    q_ref[...] += jnp.dot(normed, wq_ref[...], preferred_element_type=jnp.float32)
+    kv_ref[...] += jnp.dot(normed, wkv_ref[...], preferred_element_type=jnp.float32)
+
+
+def project(normed_all, q_cols, kv_cols):
+    _, block_len, width = normed_all.shape
+    step = min(1024, width)
+    q_wide, kv_wide = q_cols.shape[1], kv_cols.shape[1]
+    return pl.pallas_call(
+        project_kernel,
+        grid=(width // step,),
+        in_specs=[
+            pl.BlockSpec((1, block_len, step), lambda k: (0, 0, k)),
+            pl.BlockSpec((step, q_wide), lambda k: (k, 0)),
+            pl.BlockSpec((step, kv_wide), lambda k: (k, 0)),
+        ],
+        out_specs=[
+            pl.BlockSpec((block_len, q_wide), lambda k: (0, 0)),
+            pl.BlockSpec((block_len, kv_wide), lambda k: (0, 0)),
+        ],
+        out_shape=[
+            jax.ShapeDtypeStruct((block_len, q_wide), jnp.float32),
+            jax.ShapeDtypeStruct((block_len, kv_wide), jnp.float32),
+        ],
+        compiler_params=pltpu.CompilerParams(vmem_limit_bytes=32 * 1024 * 1024),
+        name="project",
+    )(normed_all, q_cols, kv_cols)
 
 
 def exchange_kernel(q_ref, kv_ref, q_all, kv_all, send, recv, own_sem):
@@ -357,10 +396,8 @@
     ).reshape(width_rows, 2 * KVH * HD)
     normed_all, q_cols, kv_cols = gather_all(fsdp_size, share_count, own_normed, w_query, wkv)
     normed_all = normed_all.reshape(4, -1, D)
-    normed = normed_all[0]
-    block_len = normed.shape[0]
-    queries = jnp.dot(normed, q_cols, preferred_element_type=jnp.float32) * inv_width
-    kv_proj = jnp.dot(normed, kv_cols, preferred_element_type=jnp.float32) * inv_width
+    block_len = normed_all.shape[1]
+    queries, kv_proj = (out * inv_width for out in project(normed_all, q_cols, kv_cols))
     key_proj, value_proj = kv_proj[:, : kv_local * HD], kv_proj[:, kv_local * HD :]
     seg_row = seg_ids[0]
     cosine_table, sine_table = angles(seg_row)

time: 489 us -> 482 us (0.986)
  matrix products: 94.2 us -> 77.6 us
  Pallas kernels: 348 us -> 364 us
  local copies, waits for them, and re-layouts: 25 us -> 16.2 us
    dot_general x2 -> x0, matrix products: 16.7 us -> none  [the longest x1 14.3 us: local(): jnp.dot(normed, q_cols, preferred_element_type=jnp.float32) * inv_width]
    pallas_call x0 -> x1, Pallas kernels: none -> 15.8 us  [project(): pl.pallas_call(project_kernel, grid=(width // step,), in_specs=[pl.BlockS...]
    slice x1 -> x0, local copies, waits for them, and re-layouts: 7.77 us -> none  [local(): normed = normed_all[0]]
    unnamed x27 -> x23, local copies, waits for them, and re-layouts: 12.4 us -> 11.4 us
where the time goes in v2:
time: 482 us; the launch traced here: 474 us
  Pallas kernels  364 us (76%)
  matrix products  77.6 us (16%)
  local copies, waits for them, and re-layouts  16.2 us (3%)
  other arithmetic  15.5 us (3%)
    pallas_call x1, Pallas kernels, gather_all(): pl.pallas_call(functools.partial(gather_kernel, count, share), out_shape=...  307 us
    dot_general x1, matrix products, local(): lax.dot_general(normed_all, all_q, contract, preferred_element_type=jnp.f...  45.1 us
    pallas_call x1, Pallas kernels, exchange(): pl.pallas_call(exchange_kernel, out_shape=(out(scaled_q), out(scaled_kv))...  41.2 us
    dot_general x1, matrix products, local(): lax.dot_general(normed_all, all_kv, contract, preferred_element_type=jnp....  17.3 us
    pallas_call x1, Pallas kernels, project(): pl.pallas_call(project_kernel, grid=(width // step,), in_specs=[pl.BlockS...  15.8 us
    unnamed x23, local copies, waits for them, and re-layouts  11.4 us

profile of v2, /device:TPU:9, one launch (start us, length us, event | category | flops | bytes accessed | tf_op | source)
XLA Modules:
  0.0 474.2 jit_solution(11689949938549597527)
XLA Ops:
  0.6 2.4 copy.57
  3.0 0.6 copy.58
  3.6 0.5 pad_maximum_fusion
  4.1 3.5 copy.59
  7.6 0.3 fusion.16
  7.9 1.2 fusion.17.n_ref
  9.1 306.6 %gather_all.1 = (bf16[4,8,64,8192]{3,2,1,0:T(8,128)(2,1)}, bf16[8192,1024]{1,0:T(8,128)(2,1)}, bf16[8192,256]{1,0:T(8,128)(2,1)}) custom-call(bf16[64,8192]{1,0:T(8,128)(2,1)} %fusion.17.n_ref, bf16[1024,8192]{1,0:T(8,128)(2,1)} %wq_ref.1, bf16[1024,2048]{1,0:T(8,128)(2,1)} %bitcast.155), custom_call_target="tpu_custom_call" | custom-call | tf_op jit(solution)/shard_map/gather_all/pallas_call | solution.py:282
  315.8 2.2 copy-done
  318.0 15.8 %project.1 = (f32[512,1024]{1,0:T(8,128)S(1)}, f32[512,256]{1,0:T(8,128)S(1)}) custom-call(bf16[4,512,8192]{2,1,0:T(8,128)(2,1)} %bitcast.150, bf16[8192,1024]{1,0:T(8,128)(2,1)} %get-tuple-element.10.wq_ref, bf16[8192,256]{1,0:T(8,128)(2,1)S(1)} %copy-done), custom_call_target="tpu_custom_call" | custom-call | tf_op jit(solution)/shard_map/project/pallas_call | solution.py:312
  333.9 0.5 copy.60
  334.4 0.7 fusion.69
  335.3 1.0 multiply_cosine_fusion
  336.3 0.8 subtract_convert_fusion
  337.2 1.4 fusion.59
  338.8 2.3 fusion.10
  341.2 1.8 fusion.9
  343.5 0.3 copy.61
  343.8 3.2 fusion.5
  346.9 2.7 fusion.11
  349.7 2.0 copy-done.2
  351.7 1.3 fusion.23
  353.0 1.2 fusion.51
  354.4 1.8 copy.52
  356.2 6.4 %fusion.30 = bf16[512,128]{1,0:T(8,128)(2,1)S(1)} fusion(f32[8,512]{1,0:T(8,128)S(1)} %fusion.9, f32[8,512]{1,0:T(8,128)S(1)} %get-tuple-element.31, f32[512,512,8]{1,0,2:T(8,128)} %copy-done.1, pred[512,512]{0,1:T(8,128)(4,1)S(1)} %fusion.38, f32[512,8,128]{0,2,1:T(8,128)} %bitcast.158, f32[512]{0:T(512)S(1)} %fusion.61), kind=kOutput, calls=%fused_computation.42 | convolution fusion | flops 548536320 | bytes 10913792 | tf_op jit(solution)/shard_map/kjqtu,tkjqd->ukjd/dot_general | solution.py:90
  362.6 0.7 pad_maximum_fusion.2.kv_ref
  363.3 1.9 multiply_bitcast_fusion
  365.3 1.0 multiply_add_fusion
  366.2 1.6 copy_bitcast_fusion.q_ref
  367.8 41.2 %exchange.1 = (bf16[4,512,1024]{2,1,0:T(8,128)(2,1)}, bf16[4,512,256]{2,1,0:T(8,128)(2,1)}) custom-call(bf16[512,1024]{1,0:T(8,128)(2,1)} %copy_bitcast_fusion.q_ref, bf16[512,256]{1,0:T(8,128)(2,1)} %pad_maximum_fusion.2.kv_ref), custom_call_target="tpu_custom_call" | custom-call | tf_op jit(solution)/shard_map/exchange/pallas_call | solution.py:365
  409.0 17.3 %fusion.4 = bf16[8192,256]{1,0:T(8,128)(2,1)S(1)} fusion(bf16[4,512,8192]{2,1,0:T(8,128)(2,1)} %bitcast.151, bf16[4,512,256]{2,1,0:T(8,128)(2,1)} %get-tuple-element.16, bf16[8192,256]{1,0:T(8,128)(2,1)} %get-tuple-element.12.wkv_ref), kind=kOutput, calls=%fused_computation.6 | convolution fusion | flops 8598323200 | bytes 42991616 | tf_op jit(solution)/shard_map/dot_general | solution.py:430
  426.4 2.3 fusion.68
  428.7 45.1 %fusion.1 = bf16[8192,1024]{1,0:T(8,128)(2,1)} fusion(bf16[8192,1024]{1,0:T(8,128)(2,1)} %get-tuple-element.10.wq_ref, bf16[4,512,8192]{2,1,0:T(8,128)(2,1)} %bitcast.152, bf16[4,512,1024]{2,1,0:T(8,128)(2,1)} %get-tuple-element.15), kind=kOutput, calls=%fused_computation.2 | convolution fusion | flops 34393292800 | bytes 71303168 | tf_op jit(solution)/shard_map/dot_general | solution.py:429
  (30 shorter events, 1.4 us)
Async XLA Ops:
  0.6 2.4 copy-start.6
  4.1 3.5 copy-start.5
  315.8 2.2 copy-start
  334.4 0.7 copy-start.7
  341.1 5.8 %copy-start.1 = (f32[512,512,8]{1,0,2:T(8,128)}, f32[512,512,8]{1,0,2:T(8,128)S(1)}, u32[]{:S(2)}) copy-start(f32[512,512,8]{1,0,2:T(8,128)S(1)} %get-tuple-element.32) | copy-start | bytes 25165828
  341.2 1.9 copy-start.8
  341.2 2.0 copy-start.4
  349.7 2.0 copy-start.2
  356.2 7.1 %copy-start.3 = (bf16[8,512,512]{1,2,0:T(8,128)(2,1)S(1)}, bf16[8,512,512]{1,2,0:T(8,128)(2,1)}, u32[]{:S(2)}) copy-start(bf16[8,512,512]{1,2,0:T(8,128)(2,1)} %copy-done.2) | copy-start | bytes 12582916
